TPU v7x, 512 devices: a whole 4x4x16 slice. The times are simulated.
512 devices in a mesh: pipe: 4 (over z_hi), dp: 16 (over y, x), tensor: 8 (over z_lo, core).
Axes of the slice: x: 4, y: 4, z: 16 (z_hi: 4, z_lo: 4; z = z_hi * 4 + z_lo), core: 2. Of those that a mesh axis runs over, the one named last changes fastest.
Arguments:
- x_in: bfloat16 [4, 2, 16, 128, 1600], P('pipe', None, 'dp', 'tensor'), may hold values from -6 to 6
- out_grad: bfloat16 [2, 16, 128, 1600], P(None, 'dp'), may hold values from -6 to 6
- layer_scale: float32 [4, 1600], P('pipe'), may hold values from 0.05 to 1
- norm_gain: float32 [4, 1600], P('pipe'), may hold values from 0.5 to 1.5
- master: float32 [4, 1600, 8192], P('pipe', 'dp', 'tensor'), may hold values from -0.15625 to 0.15625
- moment_one: float32 [4, 1600, 8192], P('pipe', 'dp', 'tensor'), may hold values from -4 to 4
- moment_two: float32 [4, 1600, 8192], P('pipe', 'dp', 'tensor'), may hold values from 0.05 to 5
Outputs:
- input_grads: bfloat16 [4, 2, 16, 128, 1600], P('pipe', None, 'dp', 'tensor')
- new_master: float32 [4, 1600, 8192], P('pipe', 'dp', 'tensor')
- new_moment_one: float32 [4, 1600, 8192], P('pipe', 'dp', 'tensor')
- new_moment_two: float32 [4, 1600, 8192], P('pipe', 'dp', 'tensor')
- scale_grads: float32 [4, 2, 1600], P('pipe')
All inputs are finite; a program needn't handle non-finite values.
Results may differ from a plain program's by a relative error of at most 0.027.
Values may be sent and summed in bfloat16 or wider, within the bound.
A program may use at most 128 MiB of HBM per device.

v0:
```python
import math
import jax
import jax.numpy as jnp
from jax import lax
from jax.sharding import PartitionSpec as P

HD = 128
beta_one = 0.9
beta_two = 0.95
adam_eps = 1e-08
learn_rate = 0.001
weight_decay = 0.05
adam_step = 100.0
norm_eps = 1e-06


def from_behind(block, axis, distance):
    devices = range(lax.axis_size(axis))
    route = [(i - distance, i) for i in devices if i - distance in devices]
    return lax.ppermute(block, axis, route)


def normalize(values_in):
    inverse = lax.rsqrt(jnp.mean(values_in * values_in, axis=-1, keepdims=True) + norm_eps)
    return (inverse, values_in * inverse)


def select_micro(array, micro_index):
    return lax.dynamic_index_in_dim(array, micro_index, 0, keepdims=False)


def store_slot(buffer, value, slot_index):
    return lax.dynamic_update_index_in_dim(buffer, value, slot_index, 0)


def local(x_in, out_grad, layer_scale, norm_gain, master, moment_one, moment_two):
    n_pipe = lax.axis_size("pipe")
    n_tensor = lax.axis_size("tensor")
    pipe_rank = lax.axis_index("pipe")
    micro_count = x_in.shape[1]
    images = x_in.shape[2]
    shard_len = x_in.shape[3]
    channels = x_in.shape[4]
    seq_len = shard_len * n_tensor
    row_start = lax.axis_index("tensor") * shard_len
    head_cols = master.shape[2] // 4
    local_heads = head_cols // HD
    score_root = math.sqrt(HD)
    scale_vec = layer_scale[0]
    gain_vec = norm_gain[0]
    weights = lax.all_gather(master[0].astype(jnp.bfloat16), "dp", axis=0, tiled=True)
    w_qkv = weights[:, : 3 * head_cols]
    w_out = weights[:, 3 * head_cols :]
    full_x = lax.all_gather(x_in[0], "tensor", axis=2, tiled=True).astype(jnp.float32)
    full_inverse, full_unit = normalize(full_x)
    normed = (full_unit * gain_vec).astype(jnp.bfloat16)
    local_unit = lax.dynamic_slice_in_dim(full_unit, row_start, shard_len, 2)
    projected = jnp.einsum(
        "mbsd,dc->mbsc", normed, w_qkv, preferred_element_type=jnp.float32
    ).astype(jnp.bfloat16)
    projected = projected.reshape(micro_count, images, seq_len, 3, local_heads, HD)
    query = projected[:, :, :, 0]
    keys = projected[:, :, :, 1]
    values = projected[:, :, :, 2]
    scores = (
        jnp.einsum("mbqhe,mbkhe->mbhqk", query, keys, preferred_element_type=jnp.float32)
        / score_root
    )
    probs = jax.nn.softmax(scores, axis=-1)
    probs_low = probs.astype(jnp.bfloat16)
    attended = jnp.einsum(
        "mbhqk,mbkhe->mbqhe", probs_low, values, preferred_element_type=jnp.float32
    ).astype(jnp.bfloat16)
    attended_flat = attended.reshape(micro_count, images, seq_len, head_cols)

    def backward_segment(micro_index, incoming):
        query_now = select_micro(query, micro_index)
        keys_now = select_micro(keys, micro_index)
        values_now = select_micro(values, micro_index)
        probs_now = select_micro(probs, micro_index)
        probs_low_now = select_micro(probs_low, micro_index)
        attended_now = select_micro(attended, micro_index)
        scaled = (scale_vec * incoming.astype(jnp.float32)).astype(jnp.bfloat16)
        d_att = jnp.einsum("bsd,dc->bsc", scaled, w_out, preferred_element_type=jnp.float32).astype(
            jnp.bfloat16
        )
        d_att = d_att.reshape(images, seq_len, local_heads, HD)
        d_prob = jnp.einsum(
            "bqhe,bkhe->bhqk", d_att, values_now, preferred_element_type=jnp.float32
        )
        row_delta = jnp.einsum(
            "bqhe,bqhe->bhq", d_att, attended_now, preferred_element_type=jnp.float32
        )
        d_score = (probs_now * (d_prob - row_delta[..., None]) / score_root).astype(jnp.bfloat16)
        d_query = jnp.einsum(
            "bhqk,bkhe->bqhe", d_score, keys_now, preferred_element_type=jnp.float32
        ).astype(jnp.bfloat16)
        d_keys = jnp.einsum(
            "bhqk,bqhe->bkhe", d_score, query_now, preferred_element_type=jnp.float32
        ).astype(jnp.bfloat16)
        d_values = jnp.einsum(
            "bhqk,bqhe->bkhe", probs_low_now, d_att, preferred_element_type=jnp.float32
        ).astype(jnp.bfloat16)
        d_proj = jnp.concatenate([d_query, d_keys, d_values], axis=2).reshape(
            images, seq_len, 3 * head_cols
        )
        partial_sum = jnp.einsum("bsc,dc->bsd", d_proj, w_qkv, preferred_element_type=jnp.float32)
        return (partial_sum, d_proj, scaled)

    def spare_segment(micro_index, incoming):
        return (
            jnp.zeros((images, seq_len, channels), jnp.float32),
            jnp.zeros((images, seq_len, 3 * head_cols), jnp.bfloat16),
            jnp.zeros((images, seq_len, channels), jnp.bfloat16),
        )

    segments = n_pipe + micro_count - 1
    is_last = pipe_rank == n_pipe - 1
    received = jnp.zeros((images, seq_len, channels), jnp.bfloat16)
    slots = micro_count + 1
    grads_out = jnp.zeros((slots, images, shard_len, channels), jnp.bfloat16)
    proj_saved = jnp.zeros((slots, images, seq_len, 3 * head_cols), jnp.bfloat16)
    scaled_saved = jnp.zeros((slots, images, seq_len, channels), jnp.bfloat16)
    grad_saved = jnp.zeros((slots, images, seq_len, channels), jnp.bfloat16)
    gain_part = jnp.zeros((channels,), jnp.float32)
    for segment_step in range(segments):
        micro_index = segment_step - (n_pipe - 1) + pipe_rank
        active = jnp.logical_and(micro_index >= 0, micro_index < micro_count)
        micro_index = jnp.clip(micro_index, 0, micro_count - 1)
        slot_index = jnp.where(active, micro_index, micro_count)
        arrived = received
        incoming = jnp.where(is_last, select_micro(out_grad, micro_index), arrived)
        partial_sum, d_proj, scaled = lax.cond(
            active, backward_segment, spare_segment, micro_index, incoming
        )
        pieces = partial_sum.astype(jnp.bfloat16).reshape(images, n_tensor, shard_len, channels)
        landed = lax.all_to_all(pieces, "tensor", split_axis=1, concat_axis=1, tiled=True)
        own_d = jnp.sum(landed.astype(jnp.float32), axis=1)
        d_normed = lax.all_gather(own_d.astype(jnp.bfloat16), "tensor", axis=1, tiled=True).astype(
            own_d.dtype
        )
        own_unit = select_micro(local_unit, micro_index)
        sel_unit = select_micro(full_unit, micro_index)
        sel_inverse = select_micro(full_inverse, micro_index)
        d_unit = d_normed * gain_vec
        d_input = sel_inverse * (
            d_unit - sel_unit * jnp.mean(d_unit * sel_unit, axis=-1, keepdims=True)
        )
        passed = (incoming.astype(jnp.float32) + d_input).astype(jnp.bfloat16)
        own_passed = lax.dynamic_slice_in_dim(passed, row_start, shard_len, 1)
        gain_part = gain_part + jnp.where(active, jnp.sum(own_d * own_unit, axis=(0, 1)), 0.0)
        grads_out = store_slot(grads_out, own_passed, slot_index)
        proj_saved = store_slot(proj_saved, d_proj, slot_index)
        scaled_saved = store_slot(scaled_saved, scaled, slot_index)
        grad_saved = store_slot(grad_saved, incoming, slot_index)
        if segment_step + 1 < segments:
            received = from_behind(passed, "pipe", -1)
    grads_kept = grads_out[:micro_count]
    proj_kept = proj_saved[:micro_count]
    scaled_kept = scaled_saved[:micro_count]
    grad_kept = grad_saved[:micro_count]
    grad_qkv = jnp.einsum("mbsd,mbsc->dc", normed, proj_kept, preferred_element_type=jnp.float32)
    grad_out = jnp.einsum(
        "mbsd,mbsc->dc", scaled_kept, attended_flat, preferred_element_type=jnp.float32
    )
    weight_grad = lax.psum_scatter(
        jnp.concatenate([grad_qkv, grad_out], axis=1).astype(jnp.bfloat16),
        "dp",
        scatter_dimension=0,
        tiled=True,
    ).astype(jnp.float32)
    summed_out = jnp.einsum(
        "mbsd,mbsc->dc", grad_kept, attended_flat, preferred_element_type=jnp.float32
    )
    scale_part = jnp.sum(w_out.astype(jnp.float32) * summed_out, axis=1)
    scale_grad, gain_grad = lax.psum((scale_part, gain_part), ("dp", "tensor"))
    bias_one = 1.0 - beta_one**adam_step
    bias_two = 1.0 - beta_two**adam_step
    first_new = beta_one * moment_one[0] + (1.0 - beta_one) * weight_grad
    second_new = beta_two * moment_two[0] + (1.0 - beta_two) * weight_grad * weight_grad
    update = first_new / bias_one / (jnp.sqrt(second_new / bias_two) + adam_eps)
    master_new = master[0] - learn_rate * (update + weight_decay * master[0])
    scale_both = jnp.stack([scale_grad, gain_grad])
    return (grads_kept[None], master_new[None], first_new[None], second_new[None], scale_both[None])


def solution(mesh):
    placed = (
        P("pipe", None, "dp", "tensor", None),
        P(None, "dp", None, None),
        P("pipe", None),
        P("pipe", None),
        P("pipe", "dp", "tensor"),
        P("pipe", "dp", "tensor"),
        P("pipe", "dp", "tensor"),
    )
    return jax.shard_map(
        local,
        mesh=mesh,
        in_specs=placed,
        out_specs=(
            P("pipe", None, "dp", "tensor", None),
            P("pipe", "dp", "tensor"),
            P("pipe", "dp", "tensor"),
            P("pipe", "dp", "tensor"),
            P("pipe", None, None),
        ),
        check_vma=False,
    )
```

profile of v0, /device:TPU:128, one launch (start us, length us, event | category | flops | bytes accessed | tf_op | source)
XLA Modules:
  0.0 1397.1 jit_solution(9497189529222593364)
XLA Ops:
  9.8 17.2 %all-gather = bf16[1,2,1,128,1600]{4,3,2,1,0:T(8,128)(2,1)S(1)} all-gather(bf16[1,2,1,16,1600]{4,3,2,1,0:T(8,128)(2,1)} %param.17), channel_id=2, replica_groups=mesh['pipe'=4,'dp'=16,'tensor'=8] {'tensor'}, dimensions={3}, use_global_device_ids=true | all-gather | bytes 921600 | tf_op jit(solution)/shard_map/all_gather | solution.py:54
  28.1 50.7 %all-gather.9.cloned.1.call-done = bf16[16,100,1024]{2,1,0:T(8,128)(2,1)} async-done(((bf16[1,100,1024]{2,1,0:T(8,128)(2,1)}), bf16[16,100,1024]{2,1,0:T(8,128)(2,1)}) %all-gather.9.cloned.1.call-update) | async-done | bytes 3276816 | tf_op jit(solution)/shard_map/all_gather | solution.py:51
  78.8 2.9 reshape.819
  81.7 3.4 fusion.113
  102.5 4.8 all-to-all-start
  111.4 2.4 copy.217
  115.1 5.5 all-to-all-done
  122.4 15.6 %all-gather.1 = bf16[128,1600]{1,0:T(8,128)(2,1)} all-gather(bf16[16,1600]{1,0:T(8,128)(2,1)S(1)} %convert_element_type.421), channel_id=3, replica_groups=mesh['pipe'=4,'dp'=16,'tensor'=8] {'tensor'}, dimensions={0}, use_global_device_ids=true | all-gather | bytes 460800 | tf_op jit(solution)/shard_map/all_gather | solution.py:139
  147.2 39.6 %collective-permute-done = bf16[1,128,1600]{1,2,0:T(8,128)(2,1)} collective-permute-done((bf16[1,128,1600]{1,2,0:T(8,128)(2,1)}, bf16[1,128,1600]{1,2,0:T(8,128)(2,1)}, u32[]{:S(2)}, u32[]{:S(2)}) %collective-permute-start) | collective-permute-done | bytes 409632 | tf_op jit(solution)/shard_map/ppermute | solution.py:20
  189.9 2.7 conditional.6
  194.6 4.1 all-to-all-start.1
  198.7 2.4 copy.231
  201.1 10.9 all-to-all-done.1
  213.7 15.6 %all-gather.2 = bf16[128,1600]{1,0:T(8,128)(2,1)} all-gather(bf16[16,1600]{1,0:T(8,128)(2,1)S(1)} %convert_element_type.429), channel_id=4, replica_groups=mesh['pipe'=4,'dp'=16,'tensor'=8] {'tensor'}, dimensions={0}, use_global_device_ids=true | all-gather | bytes 460800 | tf_op jit(solution)/shard_map/all_gather | solution.py:139
  237.3 98.2 %collective-permute-done.1 = bf16[1,128,1600]{1,2,0:T(8,128)(2,1)} collective-permute-done((bf16[1,128,1600]{1,2,0:T(8,128)(2,1)}, bf16[1,128,1600]{1,2,0:T(8,128)(2,1)}, u32[]{:S(2)}, u32[]{:S(2)}) %collective-permute-start.1) | collective-permute-done | bytes 409632 | tf_op jit(solution)/shard_map/ppermute | solution.py:20
  337.7 34.1 %conditional.7 = (bf16[1,128,1600]{1,2,0:T(8,128)(2,1)}, bf16[1,1,128,768]{3,2,0,1:T(8,128)(2,1)}, bf16[1,1,128,1600]{2,3,0,1:T(8,128)(2,1)}) conditional(s32[]{:T(128)} %convert_element_type.434, () %tuple.72, (s32[]{:T(128)}, bf16[2,1,128,2,128]{4,2,3,0,1:T(8,128)(2,1)}, f32[2,1,2,128,128]{3,4,2,0,1:T(8,128)S(1)}, f32[1,1600]{1,0:T(1,128)S(1)}, ...), branch_computations={%region_11.12_spmd, %region_12.13_spmd} | conditional | flops 454803200 | bytes 11565162 | solution.py:133
  373.8 4.1 all-to-all-start.2
  377.9 2.3 copy.245
  380.3 2.3 copy.259
  382.6 2.4 copy.273
  399.1 16.0 %all-gather.3 = bf16[128,1600]{1,0:T(8,128)(2,1)} all-gather(bf16[16,1600]{1,0:T(8,128)(2,1)S(1)} %convert_element_type.437), channel_id=5, replica_groups=mesh['pipe'=4,'dp'=16,'tensor'=8] {'tensor'}, dimensions={0}, use_global_device_ids=true | all-gather | bytes 460800 | tf_op jit(solution)/shard_map/all_gather | solution.py:139
  425.6 38.5 %collective-permute-done.2 = bf16[1,128,1600]{1,2,0:T(8,128)(2,1)S(1)} collective-permute-done((bf16[1,128,1600]{1,2,0:T(8,128)(2,1)S(1)}, bf16[1,128,1600]{1,2,0:T(8,128)(2,1)S(1)}, u32[]{:S(2)}, u32[]{:S(2)}) %collective-permute-start.2) | collective-permute-done | bytes 409632 | tf_op jit(solution)/shard_map/ppermute | solution.py:20
  465.1 34.2 %conditional.8 = (bf16[1,128,1600]{1,2,0:T(8,128)(2,1)}, bf16[1,1,128,768]{3,2,0,1:T(8,128)(2,1)}, bf16[1,1,128,1600]{2,3,0,1:T(8,128)(2,1)}) conditional(s32[]{:T(128)} %convert_element_type.442, () %tuple.74, (s32[]{:T(128)}, bf16[2,1,128,2,128]{4,2,3,0,1:T(8,128)(2,1)}, f32[2,1,2,128,128]{3,4,2,0,1:T(8,128)S(1)}, f32[1,1600]{1,0:T(1,128)S(1)}, ...), branch_computations={%region_15.16_spmd, %region_16.17_spmd} | conditional | flops 454803200 | bytes 11565162 | solution.py:133
  501.3 4.1 all-to-all-start.3
  524.3 16.0 %all-gather.4 = bf16[128,1600]{1,0:T(8,128)(2,1)} all-gather(bf16[16,1600]{1,0:T(8,128)(2,1)S(1)} %convert_element_type.445), channel_id=6, replica_groups=mesh['pipe'=4,'dp'=16,'tensor'=8] {'tensor'}, dimensions={0}, use_global_device_ids=true | all-gather | bytes 460800 | tf_op jit(solution)/shard_map/all_gather | solution.py:139
  553.3 36.9 %collective-permute-done.3 = bf16[1,128,1600]{1,2,0:T(8,128)(2,1)} collective-permute-done((bf16[1,128,1600]{1,2,0:T(8,128)(2,1)}, bf16[1,128,1600]{1,2,0:T(8,128)(2,1)}, u32[]{:S(2)}, u32[]{:S(2)}) %collective-permute-start.3) | collective-permute-done | bytes 409632 | tf_op jit(solution)/shard_map/ppermute | solution.py:20
  596.7 4.1 all-to-all-start.4
  608.2 76.2 %fusion = bf16[112,1024]{1,0:T(8,128)(2,1)} fusion(bf16[1600,1024]{1,0:T(8,128)(2,1)S(1)} %pad_maximum_fusion.5), kind=kCustom, calls=%all-reduce-scatter | all-reduce-scatter fusion | flops 1835009 | bytes 3508224
  685.4 3.7 collective-permute-start.4
  689.1 4.1 collective-permute-start.5
  703.2 15.6 %all-gather.5 = bf16[128,1600]{1,0:T(8,128)(2,1)S(1)} all-gather(bf16[16,1600]{1,0:T(8,128)(2,1)S(1)} %get-tuple-element.430), channel_id=7, replica_groups=mesh['pipe'=4,'dp'=16,'tensor'=8] {'tensor'}, dimensions={0}, use_global_device_ids=true | all-gather | bytes 460800 | tf_op jit(solution)/shard_map/all_gather | solution.py:139
  721.0 668.4 %all-reduce.2 = (f32[1,1600]{1,0:T(1,128)S(1)}, f32[1,1600]{1,0:T(1,128)S(1)}) all-reduce(f32[1,1600]{1,0:T(1,128)S(1)} %stack.10, f32[1,1600]{1,0:T(1,128)S(1)} %stack.9), channel_id=1, replica_groups=mesh['pipe'=4,'dp'=16,'tensor'=8] {'dp','tensor'}, use_global_device_ids=true, to_apply=%region_31.32 | all-reduce | flops 3200 | bytes 25600 | tf_op jit(solution)/shard_map/psum | solution.py:176
  (247 shorter events, 217.4 us)
Async XLA Ops:
  7.2 20.1 %copy-start.2 = (bf16[2,1,128,1600]{2,3,1,0:T(8,128)(2,1)S(1)}, bf16[2,1,128,1600]{2,3,1,0:T(8,128)(2,1)}, u32[]{:S(2)}) copy-start(bf16[2,1,128,1600]{2,3,1,0:T(8,128)(2,1)} %param.18) | copy-start | bytes 2457604
  7.2 71.6 %all-gather.9.cloned.1.call-start = ((), (), s32[]{:S(2)}) async-start(), calls=%async_computation.5 | async-start | bytes 3620864 | tf_op jit(solution)/shard_map/all_gather | solution.py:51
  27.3 54.4 %copy-start.44 = (f32[2,128]{1,0:T(2,128)}, f32[2,128]{1,0:T(2,128)S(1)}, u32[]{:S(2)}) copy-start(f32[2,128]{1,0:T(2,128)S(1)} %add_rsqrt_fusion) | copy-start | bytes 3076
  88.3 5.4 copy-start.34
  93.7 4.5 copy-start.42
  102.5 18.2 %all-to-all-start = ((bf16[1,8,16,1600]{3,2,0,1:T(8,128)(2,1)}), bf16[1,8,16,1600]{3,2,0,1:T(8,128)(2,1)}, u32[]{:S(2)}, u32[]{:S(2)}) async-start(bf16[1,8,16,1600]{3,2,0,1:T(8,128)(2,1)} %bitcast.535), calls=%async_computation | async-start | bytes 851968 | tf_op jit(solution)/shard_map/all_to_all | solution.py:137
  143.8 43.1 %collective-permute-start = (bf16[1,128,1600]{1,2,0:T(8,128)(2,1)}, bf16[1,128,1600]{1,2,0:T(8,128)(2,1)}, u32[]{:S(2)}, u32[]{:S(2)}) collective-permute-start(bf16[1,128,1600]{1,2,0:T(8,128)(2,1)} %fusion.145), channel_id=1, source_target_pairs={{128,0},{256,128},{384,256},{129,1},{257,129},{385,257},{130,2},{2... | collective-permute-start | bytes 1228808 | tf_op jit(solution)/shard_map/ppermute | solution.py:20
  145.9 41.0 %copy-start.3 = (bf16[2,1,128,1600]{2,3,1,0:T(8,128)(2,1)S(1)}, bf16[2,1,128,1600]{2,3,1,0:T(8,128)(2,1)}, u32[]{:S(2)}) copy-start(bf16[2,1,128,1600]{2,3,1,0:T(8,128)(2,1)} %param.18) | copy-start | bytes 2457604
  194.6 17.4 %all-to-all-start.1 = ((bf16[1,8,16,1600]{3,2,0,1:T(8,128)(2,1)}), bf16[1,8,16,1600]{3,2,0,1:T(8,128)(2,1)}, u32[]{:S(2)}, u32[]{:S(2)}) async-start(bf16[1,8,16,1600]{3,2,0,1:T(8,128)(2,1)} %bitcast.537), calls=%async_computation.1 | async-start | bytes 851968 | tf_op jit(solution)/shard_map/all_to_all | solution.py:137
  235.1 100.4 %collective-permute-start.1 = (bf16[1,128,1600]{1,2,0:T(8,128)(2,1)}, bf16[1,128,1600]{1,2,0:T(8,128)(2,1)}, u32[]{:S(2)}, u32[]{:S(2)}) collective-permute-start(bf16[1,128,1600]{1,2,0:T(8,128)(2,1)} %fusion.139), channel_id=1, source_target_pairs={{128,0},{256,128},{384,256},{129,1},{257,129},{385,257},{130,2},{2... | collective-permute-start | bytes 1228808 | tf_op jit(solution)/shard_map/ppermute | solution.py:20
  373.8 23.6 %all-to-all-start.2 = ((bf16[1,8,16,1600]{3,2,0,1:T(8,128)(2,1)}), bf16[1,8,16,1600]{3,2,0,1:T(8,128)(2,1)}, u32[]{:S(2)}, u32[]{:S(2)}) async-start(bf16[1,8,16,1600]{3,2,0,1:T(8,128)(2,1)} %bitcast.534), calls=%async_computation.2 | async-start | bytes 851968 | tf_op jit(solution)/shard_map/all_to_all | solution.py:137
  417.0 5.1 copy-start.41
  418.6 45.4 %copy-start.4 = (bf16[2,1,128,1600]{2,3,1,0:T(8,128)(2,1)S(1)}, bf16[2,1,128,1600]{2,3,1,0:T(8,128)(2,1)}, u32[]{:S(2)}) copy-start(bf16[2,1,128,1600]{2,3,1,0:T(8,128)(2,1)} %param.18) | copy-start | bytes 2457604
  420.1 45.0 %copy-start.22 = (bf16[1,128,1600]{1,2,0:T(8,128)(2,1)}, bf16[1,128,1600]{1,2,0:T(8,128)(2,1)S(1)}, u32[]{:S(2)}) copy-start(bf16[1,128,1600]{1,2,0:T(8,128)(2,1)S(1)} %fusion.133) | copy-start | bytes 1228804
  420.1 43.9 %collective-permute-start.2 = (bf16[1,128,1600]{1,2,0:T(8,128)(2,1)S(1)}, bf16[1,128,1600]{1,2,0:T(8,128)(2,1)S(1)}, u32[]{:S(2)}, u32[]{:S(2)}) collective-permute-start(bf16[1,128,1600]{1,2,0:T(8,128)(2,1)S(1)} %fusion.133), channel_id=1, source_target_pairs={{128,0},{256,128},{384,256},{129,1},{257,129},{385,257},{130,2},{2... | collective-permute-start | bytes 1228808 | tf_op jit(solution)/shard_map/ppermute | solution.py:20
  422.1 43.0 %copy-start.36 = (bf16[3,1,16,1600]{3,2,0,1:T(8,128)(2,1)}, bf16[3,1,16,1600]{3,2,0,1:T(8,128)(2,1)S(1)}, u32[]{:S(2)}) copy-start(bf16[3,1,16,1600]{3,2,0,1:T(8,128)(2,1)S(1)} %constant_dynamic-update-slice_fusion.14) | copy-start | bytes 460804
  501.3 21.3 %all-to-all-start.3 = ((bf16[1,8,16,1600]{3,2,0,1:T(8,128)(2,1)}), bf16[1,8,16,1600]{3,2,0,1:T(8,128)(2,1)}, u32[]{:S(2)}, u32[]{:S(2)}) async-start(bf16[1,8,16,1600]{3,2,0,1:T(8,128)(2,1)} %bitcast.536), calls=%async_computation.3 | async-start | bytes 851968 | tf_op jit(solution)/shard_map/all_to_all | solution.py:137
  546.1 44.2 %collective-permute-start.3 = (bf16[1,128,1600]{1,2,0:T(8,128)(2,1)}, bf16[1,128,1600]{1,2,0:T(8,128)(2,1)}, u32[]{:S(2)}, u32[]{:S(2)}) collective-permute-start(bf16[1,128,1600]{1,2,0:T(8,128)(2,1)} %fusion.127), channel_id=1, source_target_pairs={{128,0},{256,128},{384,256},{129,1},{257,129},{385,257},{130,2},{2... | collective-permute-start | bytes 1228808 | tf_op jit(solution)/shard_map/ppermute | solution.py:20
  594.7 7.8 copy-start.6
  594.7 7.8 copy-start.45
  596.7 103.9 %all-to-all-start.4 = ((bf16[1,8,16,1600]{3,2,0,1:T(8,128)(2,1)}), bf16[1,8,16,1600]{3,2,0,1:T(8,128)(2,1)}, u32[]{:S(2)}, u32[]{:S(2)}) async-start(bf16[1,8,16,1600]{3,2,0,1:T(8,128)(2,1)} %bitcast.151), calls=%async_computation.4 | async-start | bytes 851968 | tf_op jit(solution)/shard_map/all_to_all | solution.py:137
  602.5 3.8 copy-start.12
  684.4 11.5 copy-start.24
  685.4 10.5 collective-permute-start.4
  689.1 6.8 collective-permute-start.5
  697.1 4.7 copy-start.27
  697.1 4.7 copy-start.29
  697.1 4.7 copy-start.31
  697.1 4.7 copy-start.33
  700.6 18.5 %copy-start.10 = (f32[1,1,128,1600]{2,3,1,0:T(8,128)S(1)}, f32[1,1,128,1600]{2,3,1,0:T(8,128)}, u32[]{:S(2)}) copy-start(f32[1,1,128,1600]{2,3,1,0:T(8,128)} %copy.273) | copy-start | bytes 2457604
  703.2 16.3 %copy-start.17 = (bf16[1,128,1600]{1,2,0:T(8,128)(2,1)S(1)}, bf16[1,128,1600]{1,2,0:T(8,128)(2,1)}, u32[]{:S(2)}) copy-start(bf16[1,128,1600]{1,2,0:T(8,128)(2,1)} %get-tuple-element.408) | copy-start | bytes 1228804
  703.2 16.3 %copy-start.46 = (f32[16]{0:T(128)S(1)}, f32[16]{0:T(128)}, u32[]{:S(2)}) copy-start(f32[16]{0:T(128)} %dynamic-slice.8) | copy-start | bytes 196
  (19 other events, 32.5 us)
Sparse Core Ops, SparseCore 0:
  11.6 67.1 all-gather.8
where the time goes:
time: 1410 us; the launch traced here: 1400 us
  blocking collectives  840 us (60%)
  waiting for transfers between devices  281 us (20%)
  local copies, waits for them, and re-layouts  143 us (10%)
  other arithmetic  47.2 us (3%)
  starting transfers between devices  37.3 us (3%)
  matrix products  31.9 us (2%)
  between operations  15.6 us (1%)
    psum x1, blocking collectives, local(): scale_grad, gain_grad = lax.psum((scale_part, gain_part), ('dp', 'tensor'))  668 us
    ppermute x4, waiting for transfers between devices, from_behind(): return lax.ppermute(block, axis, route)  213 us
    all_gather x5, blocking collectives, local(): lax.all_gather(own_d.astype(jnp.bfloat16), 'tensor', axis=1, tiled=True)  78.7 us
    unnamed x1, blocking collectives  76.2 us
    all_gather x1, waiting for transfers between devices, local(): lax.all_gather(master[0].astype(jnp.bfloat16), 'dp', axis=0, tiled=True)  50.7 us
    another operation x23, local copies, waits for them, and re-layouts  32.1 us
  transfers between devices with their start and end apart: 12, of which 8 were waited for; matrix products, arithmetic and copies ran while one was open for 11% of the time, Pallas kernels for 0%

commit v1 on v0

--- a/solution.py
+++ b/solution.py
@@ -12,6 +12,11 @@
 weight_decay = 0.05
 adam_step = 100.0
 norm_eps = 1e-06
+
+
+def by_each_axis(value_2, first, second):
+    inner = lax.psum(value_2, first)
+    return lax.psum(inner, second)
 
 
 def from_behind(block, axis, distance):
@@ -173,7 +178,7 @@
         "mbsd,mbsc->dc", grad_kept, attended_flat, preferred_element_type=jnp.float32
     )
     scale_part = jnp.sum(w_out.astype(jnp.float32) * summed_out, axis=1)
-    scale_grad, gain_grad = lax.psum((scale_part, gain_part), ("dp", "tensor"))
+    scale_grad, gain_grad = by_each_axis((scale_part, gain_part), "tensor", "dp")
     bias_one = 1.0 - beta_one**adam_step
     bias_two = 1.0 - beta_two**adam_step
     first_new = beta_one * moment_one[0] + (1.0 - beta_one) * weight_grad

time: 1410 us -> 841 us (0.60)
  blocking collectives: 840 us -> 273 us
    psum x1 -> x2, blocking collectives: 668 us -> 101 us  [the longest x1 71.7 us: by_each_axis(): return lax.psum(inner, second)]
  transfers between devices with their start and end apart: 12 -> 12, of which waited for: 8 -> 8; matrix products, arithmetic and copies ran while one was open for 11% -> 18% of each run, Pallas kernels for 0% -> 0%
where the time goes in v1:
time: 841 us; the launch traced here: 829 us
  waiting for transfers between devices  281 us (33%)
  blocking collectives  273 us (32%)
  local copies, waits for them, and re-layouts  143 us (17%)
  other arithmetic  47.2 us (6%)
  starting transfers between devices  37.3 us (4%)
  matrix products  31.9 us (4%)
  between operations  15.6 us (2%)
    ppermute x4, waiting for transfers between devices, from_behind(): return lax.ppermute(block, axis, route)  213 us
    all_gather x5, blocking collectives, local(): lax.all_gather(own_d.astype(jnp.bfloat16), 'tensor', axis=1, tiled=True)  78.7 us
    unnamed x1, blocking collectives  76.2 us
    psum x1, blocking collectives, by_each_axis(): return lax.psum(inner, second)  71.7 us
    all_gather x1, waiting for transfers between devices, local(): lax.all_gather(master[0].astype(jnp.bfloat16), 'dp', axis=0, tiled=True)  50.7 us
    another operation x23, local copies, waits for them, and re-layouts  32.1 us
    psum x1, blocking collectives, by_each_axis(): inner = lax.psum(value_2, first)  28.9 us
    dynamic_update_slice x15, local copies, waits for them, and re-layouts, store_slot(): return lax.dynamic_update_index_in_dim(buffer, value, slot_index, 0)  21.4 us
  transfers between devices with their start and end apart: 12, of which 8 were waited for; matrix products, arithmetic and copies ran while one was open for 18% of the time, Pallas kernels for 0%

profile of v1, /device:TPU:128, one launch (start us, length us, event | category | flops | bytes accessed | tf_op | source)
XLA Modules:
  0.0 829.3 jit_solution(11837085025680797687)
XLA Ops:
  9.8 17.2 %all-gather = bf16[1,2,1,128,1600]{4,3,2,1,0:T(8,128)(2,1)S(1)} all-gather(bf16[1,2,1,16,1600]{4,3,2,1,0:T(8,128)(2,1)} %param.17), channel_id=2, replica_groups=mesh['pipe'=4,'dp'=16,'tensor'=8] {'tensor'}, dimensions={3}, use_global_device_ids=true | all-gather | bytes 921600 | tf_op jit(solution)/shard_map/all_gather | solution.py:59
  28.1 50.7 %all-gather.9.cloned.1.call-done = bf16[16,100,1024]{2,1,0:T(8,128)(2,1)} async-done(((bf16[1,100,1024]{2,1,0:T(8,128)(2,1)}), bf16[16,100,1024]{2,1,0:T(8,128)(2,1)}) %all-gather.9.cloned.1.call-update) | async-done | bytes 3276816 | tf_op jit(solution)/shard_map/all_gather | solution.py:56
  78.8 2.9 reshape.819
  81.7 3.4 fusion.113
  102.5 4.8 all-to-all-start
  111.4 2.4 copy.217
  115.1 5.5 all-to-all-done
  122.4 15.6 %all-gather.1 = bf16[128,1600]{1,0:T(8,128)(2,1)} all-gather(bf16[16,1600]{1,0:T(8,128)(2,1)S(1)} %convert_element_type.421), channel_id=3, replica_groups=mesh['pipe'=4,'dp'=16,'tensor'=8] {'tensor'}, dimensions={0}, use_global_device_ids=true | all-gather | bytes 460800 | tf_op jit(solution)/shard_map/all_gather | solution.py:144
  147.2 39.6 %collective-permute-done = bf16[1,128,1600]{1,2,0:T(8,128)(2,1)} collective-permute-done((bf16[1,128,1600]{1,2,0:T(8,128)(2,1)}, bf16[1,128,1600]{1,2,0:T(8,128)(2,1)}, u32[]{:S(2)}, u32[]{:S(2)}) %collective-permute-start) | collective-permute-done | bytes 409632 | tf_op jit(solution)/shard_map/ppermute | solution.py:25
  189.9 2.7 conditional.6
  194.6 4.1 all-to-all-start.1
  198.7 2.4 copy.231
  201.1 10.9 %all-to-all-done.1 = bf16[1,8,16,1600]{3,2,0,1:T(8,128)(2,1)} async-done(((bf16[1,8,16,1600]{3,2,0,1:T(8,128)(2,1)}), bf16[1,8,16,1600]{3,2,0,1:T(8,128)(2,1)}, u32[]{:S(2)}, u32[]{:S(2)}) %all-to-all-start.1) | async-done | bytes 409632 | tf_op jit(solution)/shard_map/all_to_all | solution.py:142
  213.7 15.6 %all-gather.2 = bf16[128,1600]{1,0:T(8,128)(2,1)} all-gather(bf16[16,1600]{1,0:T(8,128)(2,1)S(1)} %convert_element_type.429), channel_id=4, replica_groups=mesh['pipe'=4,'dp'=16,'tensor'=8] {'tensor'}, dimensions={0}, use_global_device_ids=true | all-gather | bytes 460800 | tf_op jit(solution)/shard_map/all_gather | solution.py:144
  237.3 98.2 %collective-permute-done.1 = bf16[1,128,1600]{1,2,0:T(8,128)(2,1)} collective-permute-done((bf16[1,128,1600]{1,2,0:T(8,128)(2,1)}, bf16[1,128,1600]{1,2,0:T(8,128)(2,1)}, u32[]{:S(2)}, u32[]{:S(2)}) %collective-permute-start.1) | collective-permute-done | bytes 409632 | tf_op jit(solution)/shard_map/ppermute | solution.py:25
  337.7 34.1 %conditional.7 = (bf16[1,128,1600]{1,2,0:T(8,128)(2,1)}, bf16[1,1,128,768]{3,2,0,1:T(8,128)(2,1)}, bf16[1,1,128,1600]{2,3,0,1:T(8,128)(2,1)}) conditional(s32[]{:T(128)} %convert_element_type.434, () %tuple.72, (s32[]{:T(128)}, bf16[2,1,128,2,128]{4,2,3,0,1:T(8,128)(2,1)}, f32[2,1,2,128,128]{3,4,2,0,1:T(8,128)S(1)}, f32[1,1600]{1,0:T(1,128)S(1)}, ...), branch_computations={%region_11.12_spmd, %region_12.13_spmd} | conditional | flops 454803200 | bytes 11565162 | solution.py:138
  373.8 4.1 all-to-all-start.2
  377.9 2.3 copy.245
  382.6 2.4 copy.273
  399.1 16.0 %all-gather.3 = bf16[128,1600]{1,0:T(8,128)(2,1)} all-gather(bf16[16,1600]{1,0:T(8,128)(2,1)S(1)} %convert_element_type.437), channel_id=5, replica_groups=mesh['pipe'=4,'dp'=16,'tensor'=8] {'tensor'}, dimensions={0}, use_global_device_ids=true | all-gather | bytes 460800 | tf_op jit(solution)/shard_map/all_gather | solution.py:144
  425.6 38.5 %collective-permute-done.2 = bf16[1,128,1600]{1,2,0:T(8,128)(2,1)S(1)} collective-permute-done((bf16[1,128,1600]{1,2,0:T(8,128)(2,1)S(1)}, bf16[1,128,1600]{1,2,0:T(8,128)(2,1)S(1)}, u32[]{:S(2)}, u32[]{:S(2)}) %collective-permute-start.2) | collective-permute-done | bytes 409632 | tf_op jit(solution)/shard_map/ppermute | solution.py:25
  465.1 34.2 %conditional.8 = (bf16[1,128,1600]{1,2,0:T(8,128)(2,1)}, bf16[1,1,128,768]{3,2,0,1:T(8,128)(2,1)}, bf16[1,1,128,1600]{2,3,0,1:T(8,128)(2,1)}) conditional(s32[]{:T(128)} %convert_element_type.442, () %tuple.74, (s32[]{:T(128)}, bf16[2,1,128,2,128]{4,2,3,0,1:T(8,128)(2,1)}, f32[2,1,2,128,128]{3,4,2,0,1:T(8,128)S(1)}, f32[1,1600]{1,0:T(1,128)S(1)}, ...), branch_computations={%region_15.16_spmd, %region_16.17_spmd} | conditional | flops 454803200 | bytes 11565162 | solution.py:138
  501.3 4.1 all-to-all-start.3
  524.3 16.0 %all-gather.4 = bf16[128,1600]{1,0:T(8,128)(2,1)} all-gather(bf16[16,1600]{1,0:T(8,128)(2,1)S(1)} %convert_element_type.445), channel_id=6, replica_groups=mesh['pipe'=4,'dp'=16,'tensor'=8] {'tensor'}, dimensions={0}, use_global_device_ids=true | all-gather | bytes 460800 | tf_op jit(solution)/shard_map/all_gather | solution.py:144
  553.3 36.9 %collective-permute-done.3 = bf16[1,128,1600]{1,2,0:T(8,128)(2,1)} collective-permute-done((bf16[1,128,1600]{1,2,0:T(8,128)(2,1)}, bf16[1,128,1600]{1,2,0:T(8,128)(2,1)}, u32[]{:S(2)}, u32[]{:S(2)}) %collective-permute-start.3) | collective-permute-done | bytes 409632 | tf_op jit(solution)/shard_map/ppermute | solution.py:25
  596.7 4.1 all-to-all-start.4
  608.2 76.2 %fusion = bf16[112,1024]{1,0:T(8,128)(2,1)} fusion(bf16[1600,1024]{1,0:T(8,128)(2,1)S(1)} %pad_maximum_fusion.5), kind=kCustom, calls=%all-reduce-scatter | all-reduce-scatter fusion | flops 1835009 | bytes 3508224
  685.4 3.7 collective-permute-start.4
  689.1 4.1 collective-permute-start.5
  703.2 15.6 %all-gather.5 = bf16[128,1600]{1,0:T(8,128)(2,1)S(1)} all-gather(bf16[16,1600]{1,0:T(8,128)(2,1)S(1)} %get-tuple-element.432), channel_id=7, replica_groups=mesh['pipe'=4,'dp'=16,'tensor'=8] {'tensor'}, dimensions={0}, use_global_device_ids=true | all-gather | bytes 460800 | tf_op jit(solution)/shard_map/all_gather | solution.py:144
  721.0 28.9 %all-reduce.3 = (f32[1600]{0:T(1024)S(1)}, f32[1600]{0:T(1024)S(1)}) all-reduce(f32[1600]{0:T(1024)S(1)} %select_add_fusion, f32[1600]{0:T(1024)S(1)} %fusion.112), channel_id=1, replica_groups=mesh['pipe'=4,'dp'=16,'tensor'=8] {'tensor'}, use_global_device_ids=true, to_apply=%region_32.33 | all-reduce | flops 3200 | bytes 25600 | tf_op jit(solution)/shard_map/psum | solution.py:18
  749.9 71.7 %all-reduce.2 = (f32[1,1600]{1,0:T(1,128)S(1)}, f32[1,1600]{1,0:T(1,128)S(1)}) all-reduce(f32[1,1600]{1,0:T(1,128)S(1)} %stack.10, f32[1,1600]{1,0:T(1,128)S(1)} %stack.9), channel_id=1, replica_groups=mesh['pipe'=4,'dp'=16,'tensor'=8] {'dp'}, use_global_device_ids=true, to_apply=%region_33.34 | all-reduce | flops 3200 | bytes 25600 | tf_op jit(solution)/shard_map/psum | solution.py:19
  (248 shorter events, 219.8 us)
Async XLA Ops:
  7.2 20.1 %copy-start.2 = (bf16[2,1,128,1600]{2,3,1,0:T(8,128)(2,1)S(1)}, bf16[2,1,128,1600]{2,3,1,0:T(8,128)(2,1)}, u32[]{:S(2)}) copy-start(bf16[2,1,128,1600]{2,3,1,0:T(8,128)(2,1)} %param.18) | copy-start | bytes 2457604
  7.2 71.6 %all-gather.9.cloned.1.call-start = ((), (), s32[]{:S(2)}) async-start(), calls=%async_computation.5 | async-start | bytes 3620864 | tf_op jit(solution)/shard_map/all_gather | solution.py:56
  27.3 54.4 %copy-start.44 = (f32[2,128]{1,0:T(2,128)}, f32[2,128]{1,0:T(2,128)S(1)}, u32[]{:S(2)}) copy-start(f32[2,128]{1,0:T(2,128)S(1)} %add_rsqrt_fusion) | copy-start | bytes 3076
  88.3 5.4 copy-start.34
  93.7 4.5 copy-start.42
  102.5 18.2 %all-to-all-start = ((bf16[1,8,16,1600]{3,2,0,1:T(8,128)(2,1)}), bf16[1,8,16,1600]{3,2,0,1:T(8,128)(2,1)}, u32[]{:S(2)}, u32[]{:S(2)}) async-start(bf16[1,8,16,1600]{3,2,0,1:T(8,128)(2,1)} %bitcast.535), calls=%async_computation | async-start | bytes 851968 | tf_op jit(solution)/shard_map/all_to_all | solution.py:142
  143.8 43.1 %collective-permute-start = (bf16[1,128,1600]{1,2,0:T(8,128)(2,1)}, bf16[1,128,1600]{1,2,0:T(8,128)(2,1)}, u32[]{:S(2)}, u32[]{:S(2)}) collective-permute-start(bf16[1,128,1600]{1,2,0:T(8,128)(2,1)} %fusion.145), channel_id=1, source_target_pairs={{128,0},{256,128},{384,256},{129,1},{257,129},{385,257},{130,2},{2... | collective-permute-start | bytes 1228808 | tf_op jit(solution)/shard_map/ppermute | solution.py:25
  145.9 41.0 %copy-start.3 = (bf16[2,1,128,1600]{2,3,1,0:T(8,128)(2,1)S(1)}, bf16[2,1,128,1600]{2,3,1,0:T(8,128)(2,1)}, u32[]{:S(2)}) copy-start(bf16[2,1,128,1600]{2,3,1,0:T(8,128)(2,1)} %param.18) | copy-start | bytes 2457604
  194.6 17.4 %all-to-all-start.1 = ((bf16[1,8,16,1600]{3,2,0,1:T(8,128)(2,1)}), bf16[1,8,16,1600]{3,2,0,1:T(8,128)(2,1)}, u32[]{:S(2)}, u32[]{:S(2)}) async-start(bf16[1,8,16,1600]{3,2,0,1:T(8,128)(2,1)} %bitcast.537), calls=%async_computation.1 | async-start | bytes 851968 | tf_op jit(solution)/shard_map/all_to_all | solution.py:142
  235.1 100.4 %collective-permute-start.1 = (bf16[1,128,1600]{1,2,0:T(8,128)(2,1)}, bf16[1,128,1600]{1,2,0:T(8,128)(2,1)}, u32[]{:S(2)}, u32[]{:S(2)}) collective-permute-start(bf16[1,128,1600]{1,2,0:T(8,128)(2,1)} %fusion.139), channel_id=1, source_target_pairs={{128,0},{256,128},{384,256},{129,1},{257,129},{385,257},{130,2},{2... | collective-permute-start | bytes 1228808 | tf_op jit(solution)/shard_map/ppermute | solution.py:25
  373.8 23.6 %all-to-all-start.2 = ((bf16[1,8,16,1600]{3,2,0,1:T(8,128)(2,1)}), bf16[1,8,16,1600]{3,2,0,1:T(8,128)(2,1)}, u32[]{:S(2)}, u32[]{:S(2)}) async-start(bf16[1,8,16,1600]{3,2,0,1:T(8,128)(2,1)} %bitcast.534), calls=%async_computation.2 | async-start | bytes 851968 | tf_op jit(solution)/shard_map/all_to_all | solution.py:142
  417.0 5.1 copy-start.41
  418.6 45.4 %copy-start.4 = (bf16[2,1,128,1600]{2,3,1,0:T(8,128)(2,1)S(1)}, bf16[2,1,128,1600]{2,3,1,0:T(8,128)(2,1)}, u32[]{:S(2)}) copy-start(bf16[2,1,128,1600]{2,3,1,0:T(8,128)(2,1)} %param.18) | copy-start | bytes 2457604
  420.1 45.0 %copy-start.22 = (bf16[1,128,1600]{1,2,0:T(8,128)(2,1)}, bf16[1,128,1600]{1,2,0:T(8,128)(2,1)S(1)}, u32[]{:S(2)}) copy-start(bf16[1,128,1600]{1,2,0:T(8,128)(2,1)S(1)} %fusion.133) | copy-start | bytes 1228804
  420.1 43.9 %collective-permute-start.2 = (bf16[1,128,1600]{1,2,0:T(8,128)(2,1)S(1)}, bf16[1,128,1600]{1,2,0:T(8,128)(2,1)S(1)}, u32[]{:S(2)}, u32[]{:S(2)}) collective-permute-start(bf16[1,128,1600]{1,2,0:T(8,128)(2,1)S(1)} %fusion.133), channel_id=1, source_target_pairs={{128,0},{256,128},{384,256},{129,1},{257,129},{385,257},{130,2},{2... | collective-permute-start | bytes 1228808 | tf_op jit(solution)/shard_map/ppermute | solution.py:25
  422.1 43.0 %copy-start.36 = (bf16[3,1,16,1600]{3,2,0,1:T(8,128)(2,1)}, bf16[3,1,16,1600]{3,2,0,1:T(8,128)(2,1)S(1)}, u32[]{:S(2)}) copy-start(bf16[3,1,16,1600]{3,2,0,1:T(8,128)(2,1)S(1)} %constant_dynamic-update-slice_fusion.14) | copy-start | bytes 460804
  501.3 21.3 %all-to-all-start.3 = ((bf16[1,8,16,1600]{3,2,0,1:T(8,128)(2,1)}), bf16[1,8,16,1600]{3,2,0,1:T(8,128)(2,1)}, u32[]{:S(2)}, u32[]{:S(2)}) async-start(bf16[1,8,16,1600]{3,2,0,1:T(8,128)(2,1)} %bitcast.536), calls=%async_computation.3 | async-start | bytes 851968 | tf_op jit(solution)/shard_map/all_to_all | solution.py:142
  546.1 44.2 %collective-permute-start.3 = (bf16[1,128,1600]{1,2,0:T(8,128)(2,1)}, bf16[1,128,1600]{1,2,0:T(8,128)(2,1)}, u32[]{:S(2)}, u32[]{:S(2)}) collective-permute-start(bf16[1,128,1600]{1,2,0:T(8,128)(2,1)} %fusion.127), channel_id=1, source_target_pairs={{128,0},{256,128},{384,256},{129,1},{257,129},{385,257},{130,2},{2... | collective-permute-start | bytes 1228808 | tf_op jit(solution)/shard_map/ppermute | solution.py:25
  594.7 7.8 copy-start.6
  594.7 7.8 copy-start.45
  596.7 103.9 %all-to-all-start.4 = ((bf16[1,8,16,1600]{3,2,0,1:T(8,128)(2,1)}), bf16[1,8,16,1600]{3,2,0,1:T(8,128)(2,1)}, u32[]{:S(2)}, u32[]{:S(2)}) async-start(bf16[1,8,16,1600]{3,2,0,1:T(8,128)(2,1)} %bitcast.151), calls=%async_computation.4 | async-start | bytes 851968 | tf_op jit(solution)/shard_map/all_to_all | solution.py:142
  602.5 3.8 copy-start.12
  684.4 11.5 %copy-start.24 = (bf16[112,1024]{1,0:T(8,128)(2,1)S(1)}, bf16[112,1024]{1,0:T(8,128)(2,1)}, u32[]{:S(2)}) copy-start(bf16[112,1024]{1,0:T(8,128)(2,1)} %fusion) | copy-start | bytes 688132
  685.4 10.5 %collective-permute-start.4 = (bf16[112,1024]{1,0:T(8,128)(2,1)}, bf16[112,1024]{1,0:T(8,128)(2,1)S(1)}, u32[]{:S(2)}, u32[]{:S(2)}) collective-permute-start(bf16[112,1024]{1,0:T(8,128)(2,1)} %fusion), channel_id=1, source_target_pairs={{0,8},{8,16},{16,24},{24,32},{32,40},{40,48},{48,56},{56,64},{64,7... | collective-permute-start | bytes 688136
  689.1 6.8 collective-permute-start.5
  697.1 4.7 copy-start.27
  697.1 4.7 copy-start.29
  697.1 4.7 copy-start.31
  697.1 4.7 copy-start.33
  700.6 18.5 %copy-start.10 = (f32[1,1,128,1600]{2,3,1,0:T(8,128)S(1)}, f32[1,1,128,1600]{2,3,1,0:T(8,128)}, u32[]{:S(2)}) copy-start(f32[1,1,128,1600]{2,3,1,0:T(8,128)} %copy.273) | copy-start | bytes 2457604
  703.2 16.3 %copy-start.17 = (bf16[1,128,1600]{1,2,0:T(8,128)(2,1)S(1)}, bf16[1,128,1600]{1,2,0:T(8,128)(2,1)}, u32[]{:S(2)}) copy-start(bf16[1,128,1600]{1,2,0:T(8,128)(2,1)} %get-tuple-element.410) | copy-start | bytes 1228804
  703.2 16.3 %copy-start.46 = (f32[16]{0:T(128)S(1)}, f32[16]{0:T(128)}, u32[]{:S(2)}) copy-start(f32[16]{0:T(128)} %dynamic-slice.8) | copy-start | bytes 196
  (19 other events, 32.5 us)
Sparse Core Ops, SparseCore 0:
  11.6 67.1 all-gather.8
